TPU v7x, 32 devices: a whole 2x2x4 slice. The times are simulated.
32 devices in a mesh: groups: 2 (over x), ctx: 16 (over z, y, core).
Axes of the slice: x: 2, y: 2, z: 4, core: 2. Of those that a mesh axis runs over, the one named last changes fastest.
Arguments:
- hidden_in: bfloat16 [4096, 2048], P(('groups', 'ctx')), parts along dimension 0, may hold values from -6 to 6
- queries: bfloat16 [4096, 1024], P(('groups', 'ctx')), parts along dimension 0, as said below
- keys: bfloat16 [4096, 128], P(('groups', 'ctx')), parts along dimension 0, as said below
- values: bfloat16 [4096, 128], P(('groups', 'ctx')), parts along dimension 0, may hold values from -6 to 6
- out_weight: bfloat16 [1024, 2048], replicated, may hold values from -0.5 to 0.5
- norm_gain: float32 [2048], replicated, may hold values from 0.1 to 1.9
- gate_weight: bfloat16 [2048, 11008], P(None, 'ctx'), may hold values from -0.125 to 0.125
- up_weight: bfloat16 [2048, 11008], P(None, 'ctx'), may hold values from -0.125 to 0.125
- down_weight: bfloat16 [11008, 2048], P('ctx'), may hold values from -0.0546875 to 0.0546875
- pair_ids: int32 [4096], P('groups'), parts along dimension 0, may hold values from 0 to 3, as said below
- roles: int32 [4096], P('groups'), parts along dimension 0, may hold values from 0 to 2, as said below
- send_rows: int32 [32, 128], P(('groups', 'ctx')), parts along dimension 0, may hold values from 0 to 127, as said below
- send_counts: int32 [32, 16], P('groups'), parts along dimension 0, may hold values from 0 to 8, as said below
Outputs:
- layer_out: bfloat16 [4096, 2048], P(('groups', 'ctx')), parts along dimension 0
There are 2 independent parts, one for each index of `groups`. A program takes and returns all parts, laid end to end along the dimension named above; an argument that names none is the same for every part. Nothing has to cross between parts.
Inputs may be any that keep to these rules, and one draw needn't show every extreme that they name: `pair_ids`: never falls along the sequence; every pair is present, and one pair's chosen response spans 256 positions or more. `roles`: each pair is a prompt, then its chosen response, then its rejected response, each of one position or more; responses fill exactly 1536 positions. `send_rows`: slots j * 8 + k with k < send_counts[i, j] list distinct local rows of device i, together exactly its positions whose role is not 0; other slots hold 0. `send_counts`: replicated on every device; every column sums to 96; some entry equals 8. `queries`: values within -8 to 8. `keys`: values within -8 to 8.
All inputs are finite; a program needn't handle non-finite values.
Results may differ from a plain program's by a relative error of at most 0.015.
Values may be sent and summed in bfloat16 or wider, within the bound.
No kernel may reach another device: no remote copies, remote signals or barrier semaphores. Data moves between devices by JAX's collectives and lax.ppermute only.
A program may use at most 128 MiB of HBM per device.

v0:
```python
import jax
import jax.numpy as jnp
from jax import lax
from jax.sharding import PartitionSpec as P

NEG_FILL = -1e30


def on_device(
    hidden_in,
    queries,
    keys,
    values,
    out_weight,
    norm_gain,
    gate_weight,
    up_weight,
    down_weight,
    pair_ids,
    roles,
    send_rows,
    send_counts,
):
    devices = lax.axis_size("ctx")
    my_index = lax.axis_index("ctx")
    tok_rows = hidden_in.shape[0]
    head_dim = keys.shape[1]
    head_count = queries.shape[1] // head_dim
    own_begin = my_index * tok_rows
    query_pos = own_begin + jnp.arange(tok_rows, dtype=jnp.int32)
    query_pair = lax.dynamic_slice_in_dim(pair_ids, own_begin, tok_rows)
    query_role = lax.dynamic_slice_in_dim(roles, own_begin, tok_rows)
    query_heads = queries.reshape(tok_rows, head_count, head_dim)
    score_scale = 1.0 / head_dim**0.5
    key_piece = lax.all_gather(keys, "ctx", axis=0, tiled=True)
    value_piece = lax.all_gather(values, "ctx", axis=0, tiled=True)
    row_count = key_piece.shape[0]
    key_pos = jnp.arange(row_count, dtype=jnp.int32)
    seen_mask = (
        (query_pair[:, None] == pair_ids[None, :])
        & (key_pos[None, :] <= query_pos[:, None])
        & ((roles[None, :] == 0) | (roles[None, :] == query_role[:, None]))
    )
    maximum = jnp.full((head_count, tok_rows), NEG_FILL, jnp.float32)
    scores = (
        jnp.einsum("tqd,kd->qtk", query_heads, key_piece, preferred_element_type=jnp.float32)
        * score_scale
    )
    masked = jnp.where(seen_mask[None], scores, NEG_FILL)
    fresh_max = jnp.maximum(maximum, jnp.max(masked, axis=-1))
    weights = jnp.where(seen_mask[None], jnp.exp(masked - fresh_max[..., None]), 0.0)
    denominator = jnp.sum(weights, axis=-1)
    numerator = jnp.einsum(
        "qtk,kd->qtd", weights.astype(jnp.bfloat16), value_piece, preferred_element_type=jnp.float32
    )
    maximum, denominator, numerator = (fresh_max, denominator, numerator)
    attention = (
        (numerator / denominator[..., None])
        .transpose(1, 0, 2)
        .reshape(tok_rows, head_count * head_dim)
        .astype(jnp.bfloat16)
    )
    residual = (
        hidden_in.astype(jnp.float32)
        + jnp.dot(attention, out_weight, preferred_element_type=jnp.float32)
    ).astype(jnp.bfloat16)
    wide = residual.astype(jnp.float32)
    mean_sq = jnp.mean(wide * wide, axis=-1, keepdims=True)
    normed = (wide * lax.rsqrt(mean_sq + 1e-06) * norm_gain[None, :]).astype(jnp.bfloat16)
    slot_total = send_rows.shape[1]
    capacity = slot_total // devices
    rows_flat = send_rows[0]
    my_counts = lax.dynamic_slice_in_dim(send_counts, my_index, 1, 0)[0]
    valid = jnp.tile(jnp.arange(capacity, dtype=jnp.int32), devices) < jnp.repeat(
        my_counts, capacity
    )
    target = jnp.where(valid, rows_flat, tok_rows)
    gathered = lax.all_gather(normed, "ctx", axis=0, tiled=True)
    gate_out = jnp.dot(gathered, gate_weight, preferred_element_type=jnp.float32)
    up_out = jnp.dot(gathered, up_weight, preferred_element_type=jnp.float32)
    inner_out = (jax.nn.silu(gate_out) * up_out).astype(jnp.bfloat16)
    summed = lax.psum_scatter(
        jnp.dot(inner_out, down_weight, preferred_element_type=jnp.float32).astype(jnp.bfloat16),
        "ctx",
        scatter_dimension=0,
        tiled=True,
    )
    live_mask = jnp.zeros((tok_rows,), jnp.float32).at[target].set(1.0, mode="drop")
    ffn_round = lax.optimization_barrier(summed)
    ffn_back = ffn_round.astype(jnp.float32) * live_mask[:, None]
    return (residual.astype(jnp.float32) + ffn_back).astype(jnp.bfloat16)


def solution(mesh):
    return jax.shard_map(
        on_device,
        mesh=mesh,
        in_specs=(
            P(("groups", "ctx"), None),
            P(("groups", "ctx"), None),
            P(("groups", "ctx"), None),
            P(("groups", "ctx"), None),
            P(),
            P(),
            P(None, "ctx"),
            P(None, "ctx"),
            P("ctx", None),
            P("groups"),
            P("groups"),
            P(("groups", "ctx"), None),
            P("groups", None),
        ),
        out_specs=P(("groups", "ctx"), None),
        check_vma=False,
    )
```

profile of v0, /device:TPU:0, one launch (start us, length us, event | category | flops | bytes accessed | tf_op | source)
XLA Modules:
  0.0 281.5 jit_solution(8424827407678132025)
XLA Ops:
  6.5 0.0 copy-start
  6.5 0.0 all-gather.2.cloned.1.call-start
  6.5 0.9 broadcast_compare_fusion
  7.4 0.8 dynamic_slice.10
  8.2 0.8 dynamic_slice.9
  8.9 0.9 copy.18
  9.8 24.6 %all_gather.10 = bf16[2048,128]{0,1:T(8,128)(2,1)S(1)} all-gather(bf16[128,128]{0,1:T(8,128)(2,1)S(1)} %copy.18), channel_id=1, replica_groups=mesh['groups'=2,'ctx'=16] {'ctx'}, dimensions={0}, use_global_device_ids=true | all-gather | bytes 557056 | tf_op jit(solution)/shard_map/all_gather | solution.py:36
  34.4 19.1 %all_gather.9 = bf16[2048,128]{1,0:T(8,128)(2,1)S(1)} all-gather(bf16[128,128]{1,0:T(8,128)(2,1)} %param.15), channel_id=1, replica_groups=mesh['groups'=2,'ctx'=16] {'ctx'}, dimensions={0}, use_global_device_ids=true | all-gather | bytes 557056 | tf_op jit(solution)/shard_map/all_gather | solution.py:35
  53.5 3.1 %fusion.13 = pred[128,2048]{0,1:T(8,128)(4,1)S(1)} fusion(s32[128]{0:T(128)S(1)} %dynamic_slice.10, s32[128]{0:T(128)S(1)} %iota_add_fusion, s32[128]{0:T(128)S(1)} %dynamic_slice.9, s32[2048]{0:T(1024)} %param.23, s32[2048]{0:T(1024)} %param.22, pred[2048]{0:T(1024)(128)(4,1)S(1)} %broadcast_compare_fusion), kind=kLoop, calls=%fused_computation.20 | loop fusion | flops 1572864 | bytes 282112 | tf_op jit(solution)/shard_map/and | solution.py:40
  56.5 2.3 fusion
  58.9 2.0 fusion.1
  60.9 0.0 copy-start.2
  60.9 0.0 copy-start.3
  60.9 0.0 copy-start.4
  60.9 2.2 fusion.17
  63.2 0.0 copy-done.2
  63.2 0.0 copy-done.3
  63.2 0.8 multiply_reduce_fusion
  64.0 1.0 copy-done.1
  65.0 1.0 multiply_convert_fusion.1
  66.0 0.0 all-gather.2.cloned.1.call-update
  66.0 0.2 reduce-scatter.2.cloned.1.call-start
  66.2 73.2 %all-gather.2.cloned.1.call-done = bf16[2048,2048]{1,0:T(8,128)(2,1)} async-done(((bf16[128,2048]{1,0:T(8,128)(2,1)}), bf16[2048,2048]{1,0:T(8,128)(2,1)}) %all-gather.2.cloned.1.call-update) | async-done | bytes 8388624 | tf_op jit(solution)/shard_map/all_gather | solution.py:78
  139.4 11.0 %fusion.32 = f32[2048,688]{0,1:T(8,128)} fusion(bf16[2048,2048]{1,0:T(8,128)(2,1)} %all-gather.2.cloned.1.call-done, bf16[2048,688]{0,1:T(8,128)(2,1)} %param.19), kind=kOutput, calls=%fused_computation.43 | convolution fusion | flops 5771362304 | bytes 16842752 | tf_op jit(solution)/shard_map/dot_general | solution.py:79
  150.4 18.9 %convolution_convert_fusion = bf16[2048,2048]{1,0:T(8,128)(2,1)} fusion(bf16[688,2048]{1,0:T(8,128)(2,1)S(1)} %copy-done, f32[2048,688]{0,1:T(8,128)} %fusion.32, bf16[2048,2048]{1,0:T(8,128)(2,1)} %all-gather.2.cloned.1.call-done, bf16[2048,688]{0,1:T(8,128)(2,1)} %param.20), kind=kOutput, calls=%fused_computation.3 | convolution fusion | flops 11555373056 | bytes 28049408 | tf_op jit(solution)/shard_map/dot_general | solution.py:83
  169.3 0.0 reduce-scatter.2.cloned.1.call-update
  169.3 0.7 dynamic-slice_bitcast_fusion
  170.0 0.1 iota_compare_fusion.1
  170.1 0.1 lt.36
  170.2 1.0 scatter_custom_fusion
  171.2 101.1 %reduce-scatter.2.cloned.1.call-done = bf16[128,2048]{1,0:T(8,128)(2,1)} async-done(((bf16[2048,2048]{1,0:T(8,128)(2,1)}), bf16[128,2048]{1,0:T(8,128)(2,1)}) %reduce-scatter.2.cloned.1.call-update) | async-done | bytes 524304 | tf_op jit(solution)/shard_map/reduce_scatter | solution.py:82
  272.3 2.3 add_convert_fusion
  (10 shorter events, 0.0 us)
Async XLA Ops:
  6.5 143.9 %copy-start = (bf16[688,2048]{1,0:T(8,128)(2,1)S(1)}, bf16[688,2048]{1,0:T(8,128)(2,1)}, u32[]{:S(2)}) copy-start(bf16[688,2048]{1,0:T(8,128)(2,1)} %param.21) | copy-start | bytes 8454148
  6.5 132.9 %all-gather.2.cloned.1.call-start = ((), (), s32[]{:S(2)}) async-start(), calls=%async_computation.1 | async-start | bytes 8912896 | tf_op jit(solution)/shard_map/all_gather | solution.py:78
  60.9 2.3 copy-start.2
  60.9 2.3 copy-start.3
  60.9 4.1 %copy-start.4 = (f32[2048]{0:T(1024)S(1)}, f32[2048]{0:T(1024)}, u32[]{:S(2)}) copy-start(f32[2048]{0:T(1024)} %param.18) | copy-start | bytes 24580
  64.0 1.0 copy-start.1
  66.0 206.3 %reduce-scatter.2.cloned.1.call-start = ((), (), s32[]{:S(2)}) async-start(), calls=%async_computation.2 | async-start | bytes 8912896 | tf_op jit(solution)/shard_map/reduce_scatter | solution.py:82
  169.3 0.9 copy-start.5
Sparse Core Ops, SparseCore 0:
  66.1 73.2 all-gather.1
  169.4 102.8 reduce-scatter.1
where the time goes:
time: 282 us; the launch traced here: 281 us
  waiting for transfers between devices  174 us (62%)
  blocking collectives  43.7 us (15%)
  matrix products  35.2 us (12%)
  between operations  13.5 us (5%)
  other arithmetic  9.31 us (3%)
  local copies, waits for them, and re-layouts  5.19 us (2%)
    reduce_scatter x1, waiting for transfers between devices, on_device(): lax.psum_scatter(jnp.dot(inner_out, down_weight, preferred_element_type=j...  101 us
    all_gather x1, waiting for transfers between devices, on_device(): gathered = lax.all_gather(normed, 'ctx', axis=0, tiled=True)  73.2 us
    all_gather x1, blocking collectives, on_device(): value_piece = lax.all_gather(values, 'ctx', axis=0, tiled=True)  24.6 us
    all_gather x1, blocking collectives, on_device(): key_piece = lax.all_gather(keys, 'ctx', axis=0, tiled=True)  19.1 us
    dot_general x1, matrix products, on_device(): jnp.dot(inner_out, down_weight, preferred_element_type=jnp.float32)  18.9 us
    dot_general x1, matrix products, on_device(): jnp.dot(gathered, gate_weight, preferred_element_type=jnp.float32)  11 us
  transfers between devices with their start and end apart: 2, of which 2 were waited for; matrix products, arithmetic and copies ran while one was open for 1% of the time, Pallas kernels for 0%

commit v1 on v0

v1 whole, which is shorter than its diff:
```python
import functools
import math

import jax
import jax.numpy as jnp
import numpy as np
from jax import lax
from jax.experimental import pallas as pl
from jax.experimental.pallas import tpu as pltpu
from jax.sharding import PartitionSpec as P

NEG_FILL = -1e30
CORES = 2
PLANE = 4
MIB = 1 << 20


class Ring:
    def __init__(self, groups, devices):
        chips = devices // CORES
        columns = max(1, PLANE // groups)
        if chips % columns:
            columns = 1
        depth = chips // columns
        order = []
        for column in range(columns):
            line = [level * columns + column for level in range(depth)]
            order += line if column % 2 == 0 else line[::-1]
        self.chips = chips
        self.half = chips // 2
        self.order = order
        self.swap = [(i, i ^ 1) for i in range(devices)]

    def go(self, block, hops):
        pairs = []
        for place in range(self.chips):
            here, there = self.order[place], self.order[(place + hops) % self.chips]
            pairs += [(here * CORES + core, there * CORES + core) for core in range(CORES)]
        return lax.ppermute(block, "ctx", pairs)

    def go_mate(self, block):
        return lax.ppermute(block, "ctx", self.swap)

    def owners(self, spots):
        place_of = {chip: place for place, chip in enumerate(self.order)}
        table = []
        for device in range(self.chips * CORES):
            chip, core = divmod(device, CORES)
            own = [
                self.order[(place_of[chip] + spot) % self.chips] * CORES + core for spot in spots
            ]
            table.append(own + [d ^ 1 for d in own])
        return np.asarray(table, np.int32)


def attention_kernel(
    count,
    heads,
    head_dim,
    owner_ref,
    edge_ref,
    query_ref,
    hidden_ref,
    gain_ref,
    pair_ref,
    role_ref,
    out_weight_hbm,
    *refs,
):
    keys, values = refs[:count], refs[count : 2 * count]
    (residual_ref, normed_ref, weight_ref, stacked, scores, top, total, summed, sem) = refs[
        2 * count :
    ]
    rows = query_ref.shape[0]
    fetch = pltpu.make_async_copy(out_weight_hbm, weight_ref, sem)
    fetch.start()
    me = owner_ref[0]
    for head in range(heads):
        stacked[pl.ds(head * rows, rows), :] = query_ref[:, head * head_dim : (head + 1) * head_dim]

    def column(ref):
        return jnp.broadcast_to(ref[pl.ds(me, 1), :], (rows, rows)).T

    query_pair, query_role = column(pair_ref), column(role_ref)
    query_pos = me * rows + lax.broadcasted_iota(jnp.int32, (rows, rows), 0)
    key_off = lax.broadcasted_iota(jnp.int32, (rows, rows), 1)

    def needed(owner):
        first_pair, last_pair = edge_ref[owner, 0], edge_ref[owner, 1]
        first_role, last_role = edge_ref[owner, 2], edge_ref[owner, 3]
        my_first, my_last = edge_ref[me, 0], edge_ref[me, 1]
        apart = (
            (first_pair == last_pair)
            & (my_first == my_last)
            & (first_role == last_role)
            & (edge_ref[me, 2] == edge_ref[me, 3])
            & (first_role != 0)
            & (first_role != edge_ref[me, 2])
        )
        return (owner <= me) & (last_pair >= my_first) & jnp.logical_not(apart)

    top[...] = jnp.full_like(top, NEG_FILL)
    total[...] = jnp.zeros_like(total)
    summed[...] = jnp.zeros_like(summed)
    for j in range(count):
        owner = owner_ref[j]

        @pl.when(needed(owner))
        def _():
            seen = (
                (query_pair == pair_ref[pl.ds(owner, 1), :])
                & (owner * rows + key_off <= query_pos)
                & (
                    (role_ref[pl.ds(owner, 1), :] == 0)
                    | (role_ref[pl.ds(owner, 1), :] == query_role)
                )
            )
            bias = jnp.where(seen, 0.0, NEG_FILL)
            raw = lax.dot_general(
                stacked[...],
                keys[j][...],
                (((1,), (1,)), ((), ())),
                preferred_element_type=jnp.float32,
            )
            masked = raw.reshape(heads, rows, rows) + bias[None]
            scores[j] = masked
            top[...] = jnp.maximum(top[...], masked)

    top[...] = jnp.broadcast_to(jnp.max(top[...], axis=-1, keepdims=True), top.shape)
    factor = math.log2(math.e) / math.sqrt(head_dim)
    for j in range(count):
        owner = owner_ref[j]

        @pl.when(needed(owner))
        def _():
            weights = jnp.exp2((scores[j] - top[...]) * factor)
            total[...] += weights
            summed[...] += jnp.dot(
                weights.astype(jnp.bfloat16).reshape(heads * rows, rows),
                values[j][...],
                preferred_element_type=jnp.float32,
            ).reshape(heads, rows, head_dim)

    mixed = (summed[...] / jnp.sum(total[...], axis=-1, keepdims=True)).astype(jnp.bfloat16)
    mixed = jnp.concatenate([mixed[head] for head in range(heads)], axis=1)
    fetch.wait()
    projected = jnp.dot(mixed, weight_ref[...], preferred_element_type=jnp.float32)
    residual = (hidden_ref[...].astype(jnp.float32) + projected).astype(jnp.bfloat16)
    residual_ref[...] = residual
    wide = residual.astype(jnp.float32)
    mean_sq = jnp.mean(wide * wide, axis=-1, keepdims=True)
    normed_ref[...] = (wide * lax.rsqrt(mean_sq + 1e-06) * gain_ref[...]).astype(jnp.bfloat16)


def attend(owners, queries, hidden, gain, pair_ids, roles, out_weight, keys, values):
    rows, width = queries.shape
    head_dim = keys[0].shape[1]
    heads = width // head_dim
    count = len(keys)
    pairs = pair_ids.reshape(-1, rows)
    parts = roles.reshape(-1, rows)
    edges = jnp.stack([pairs[:, 0], pairs[:, -1], parts[:, 0], parts[:, -1]], axis=1)
    smem = pl.BlockSpec(memory_space=pltpu.SMEM)
    vmem = pl.BlockSpec(memory_space=pltpu.VMEM)
    square = pltpu.VMEM((heads, rows, rows), jnp.float32)
    return pl.pallas_call(
        functools.partial(attention_kernel, count, heads, head_dim),
        out_shape=(
            jax.ShapeDtypeStruct(hidden.shape, jnp.bfloat16),
            jax.ShapeDtypeStruct(hidden.shape, jnp.bfloat16),
        ),
        in_specs=[smem, smem]
        + [vmem] * 5
        + [pl.BlockSpec(memory_space=pl.ANY)]
        + [vmem] * (2 * count),
        out_specs=(vmem, vmem),
        scratch_shapes=[
            pltpu.VMEM(out_weight.shape, jnp.bfloat16),
            pltpu.VMEM((heads * rows, head_dim), jnp.bfloat16),
            pltpu.VMEM((count, heads, rows, rows), jnp.float32),
            square,
            square,
            pltpu.VMEM((heads, rows, head_dim), jnp.float32),
            pltpu.SemaphoreType.DMA,
        ],
        compiler_params=pltpu.CompilerParams(vmem_limit_bytes=48 * MIB),
        name="attention",
    )(
        owners,
        edges,
        queries,
        hidden,
        gain.reshape(1, -1),
        pairs,
        parts,
        out_weight,
        *keys,
        *values,
    )


def ffn_kernel(blocks, sizes, *refs):
    inputs, refs = refs[:blocks], refs[blocks:]
    weights_hbm, refs = refs[:6], refs[6:]
    outputs, refs = refs[:blocks], refs[blocks:]
    weights, (total, sems) = refs[:6], refs[6:]
    fetches = []
    for k in range(6):
        fetches.append(pltpu.make_async_copy(weights_hbm[k], weights[k], sems.at[k]))
        fetches[k].start()
    block = jnp.concatenate([ref[...] for ref in inputs], axis=0)
    for side in range(2):
        gate, up, down = weights[3 * side : 3 * side + 3]
        fetches[3 * side].wait()
        gate_out = jnp.dot(block, gate[...], preferred_element_type=jnp.float32)
        fetches[3 * side + 1].wait()
        up_out = jnp.dot(block, up[...], preferred_element_type=jnp.float32)
        inner = (gate_out / (1.0 + jnp.exp(-gate_out)) * up_out).astype(jnp.bfloat16)
        fetches[3 * side + 2].wait()
        part = jnp.dot(inner, down[...], preferred_element_type=jnp.float32)
        if side == 0:
            total[...] = part
        else:
            part = part + total[...]
            begin = 0
            for ref, size in zip(outputs, sizes):
                ref[...] = part[begin : begin + size].astype(jnp.bfloat16)
                begin += size


def ffn(blocks, weights):
    sizes = [b.shape[0] for b in blocks]
    width = blocks[0].shape[1]
    vmem = pl.BlockSpec(memory_space=pltpu.VMEM)
    flops = 2 * sum(sizes) * sum(w.size for w in weights)
    return pl.pallas_call(
        functools.partial(ffn_kernel, len(blocks), sizes),
        out_shape=tuple(jax.ShapeDtypeStruct(b.shape, jnp.bfloat16) for b in blocks),
        in_specs=[vmem] * len(blocks) + [pl.BlockSpec(memory_space=pl.ANY)] * 6,
        out_specs=(vmem,) * len(blocks),
        scratch_shapes=[pltpu.VMEM(w.shape, w.dtype) for w in weights]
        + [pltpu.VMEM((sum(sizes), width), jnp.float32), pltpu.SemaphoreType.DMA((6,))],
        compiler_params=pltpu.CompilerParams(vmem_limit_bytes=48 * MIB),
        cost_estimate=pl.CostEstimate(
            flops=flops,
            transcendentals=0,
            bytes_accessed=2 * sum(w.size for w in weights),
        ),
        name="feed_forward",
    )(*blocks, *weights)


def feed_forward(ring, normed, weights):
    mid = normed.shape[0] // 2
    fwd, bwd = [normed], [normed]
    for _ in range(1, ring.half):
        fwd.append(ring.go(fwd[-1], 1))
        bwd.append(ring.go(bwd[-1], -1))
    far_fwd = ring.go(fwd[-1][:mid], 1)
    far_bwd = ring.go(bwd[-1][mid:], -1)
    (own_term,) = ffn((normed,), weights)
    terms = [None]
    for step in range(1, ring.half):
        terms.append(ffn((fwd[step], bwd[step]), weights))
    far_terms = ffn((far_fwd, far_bwd), weights)

    def add(a, b):
        return (a.astype(jnp.float32) + b.astype(jnp.float32)).astype(jnp.bfloat16)

    home_bwd = ring.go(far_terms[0], -1)
    home_fwd = ring.go(far_terms[1], 1)
    for step in range(ring.half - 1, 0, -1):
        term_bwd, term_fwd = terms[step]
        if step == ring.half - 1:
            home_bwd = jnp.concatenate([add(home_bwd, term_bwd[:mid]), term_bwd[mid:]], axis=0)
            home_fwd = jnp.concatenate([term_fwd[:mid], add(home_fwd, term_fwd[mid:])], axis=0)
        else:
            home_bwd, home_fwd = add(home_bwd, term_bwd), add(home_fwd, term_fwd)
        home_bwd = ring.go(home_bwd, -1)
        home_fwd = ring.go(home_fwd, 1)
    return (
        own_term.astype(jnp.float32) + home_bwd.astype(jnp.float32) + home_fwd.astype(jnp.float32)
    )


def gather_kv(ring, keys, values):
    spots = [0]
    all_keys, all_values = [keys], [values]
    for hops in range(1, ring.half):
        for way in (1, -1):
            spots.append(-way * hops)
            all_keys.append(ring.go(keys, way * hops))
            all_values.append(ring.go(values, way * hops))
    spots.append(ring.half)
    all_keys.append(ring.go(keys, ring.half))
    all_values.append(ring.go(values, -ring.half))
    all_keys += [ring.go_mate(block) for block in all_keys]
    all_values += [ring.go_mate(block) for block in all_values]
    return spots, all_keys, all_values


def on_device(
    ring,
    hidden_in,
    queries,
    keys,
    values,
    out_weight,
    norm_gain,
    gate_weight,
    up_weight,
    down_weight,
    pair_ids,
    roles,
    send_rows,
    send_counts,
):
    my_index = lax.axis_index("ctx")
    tok_rows = hidden_in.shape[0]
    own = (gate_weight, up_weight, down_weight)
    weights = own + tuple(ring.go_mate(w) for w in own)

    spots, all_keys, all_values = gather_kv(ring, keys, values)
    owners = jnp.asarray(ring.owners(spots))[my_index]
    residual, normed = attend(
        owners, queries, hidden_in, norm_gain, pair_ids, roles, out_weight, all_keys, all_values
    )
    summed = feed_forward(ring, normed, weights)
    my_roles = lax.dynamic_slice_in_dim(roles, my_index * tok_rows, tok_rows)
    live = (my_roles != 0).astype(jnp.float32)
    ffn_back = summed.astype(jnp.bfloat16).astype(jnp.float32) * live[:, None]
    return (residual.astype(jnp.float32) + ffn_back).astype(jnp.bfloat16)


def solution(mesh):
    ring = Ring(mesh.shape["groups"], mesh.shape["ctx"])

    def run(*arrays):
        return on_device(ring, *arrays)

    return jax.shard_map(
        run,
        mesh=mesh,
        in_specs=(
            P(("groups", "ctx"), None),
            P(("groups", "ctx"), None),
            P(("groups", "ctx"), None),
            P(("groups", "ctx"), None),
            P(),
            P(),
            P(None, "ctx"),
            P(None, "ctx"),
            P("ctx", None),
            P("groups"),
            P("groups"),
            P(("groups", "ctx"), None),
            P("groups", None),
        ),
        out_specs=P(("groups", "ctx"), None),
        check_vma=False,
    )
```

time: 282 us -> 191 us (0.68)
  waiting for transfers between devices: 174 us -> 67.3 us
  Pallas kernels: 0 us -> 44 us
  blocking collectives: 43.7 us -> 0 us
  starting transfers between devices: 0.22 us -> 43.2 us
  matrix products: 35.2 us -> 0 us
  local copies, waits for them, and re-layouts: 5.19 us -> 29.6 us
  between operations: 13.5 us -> 0.28 us
  other arithmetic: 9.31 us -> 5.55 us
    reduce_scatter x1 -> x0, waiting for transfers between devices: 101 us -> none  [on_device(): lax.psum_scatter(jnp.dot(inner_out, down_weight, preferred_element_type=j...]
    all_gather x1 -> x0, waiting for transfers between devices: 73.2 us -> none  [on_device(): gathered = lax.all_gather(normed, 'ctx', axis=0, tiled=True)]
    ppermute x0 -> x49, waiting for transfers between devices: none -> 67.3 us  [the longest x30 62.6 us: go(): return lax.ppermute(block, 'ctx', pairs)]
    pallas_call x0 -> x6, Pallas kernels: none -> 44 us  [the longest x5 40.1 us: ffn(): pl.pallas_call(functools.partial(ffn_kernel, len(blocks), sizes), out_sha...]
    all_gather x2 -> x0, blocking collectives: 43.7 us -> none  [the longest x1 24.6 us: on_device(): value_piece = lax.all_gather(values, 'ctx', axis=0, tiled=True)]
    ppermute x0 -> x49, starting transfers between devices: none -> 43.2 us  [the longest x30 38.5 us: go(): return lax.ppermute(block, 'ctx', pairs)]
    dot_general x5 -> x0, matrix products: 35.2 us -> none  [the longest x1 18.9 us: on_device(): jnp.dot(inner_out, down_weight, preferred_element_type=jnp.float32)]
    unnamed x13 -> x48, local copies, waits for them, and re-layouts: 1.89 us -> 17.2 us
  transfers between devices with their start and end apart: 2 -> 49, of which waited for: 2 -> 23; matrix products, arithmetic and copies ran while one was open for 1% -> 12% of each run, Pallas kernels for 0% -> 19%
where the time goes in v1:
time: 191 us; the launch traced here: 190 us
  waiting for transfers between devices  67.3 us (35%)
  Pallas kernels  44 us (23%)
  starting transfers between devices  43.2 us (23%)
  local copies, waits for them, and re-layouts  29.6 us (15%)
  other arithmetic  5.55 us (3%)
    ppermute x30, waiting for transfers between devices, go(): return lax.ppermute(block, 'ctx', pairs)  62.6 us
    pallas_call x5, Pallas kernels, ffn(): pl.pallas_call(functools.partial(ffn_kernel, len(blocks), sizes), out_sha...  40.1 us
    ppermute x30, starting transfers between devices, go(): return lax.ppermute(block, 'ctx', pairs)  38.5 us
    unnamed x48, local copies, waits for them, and re-layouts  17.2 us
    ppermute x2, local copies, waits for them, and re-layouts, go_mate(): return lax.ppermute(block, 'ctx', self.swap)  9.4 us
    ppermute x19, starting transfers between devices, go_mate(): return lax.ppermute(block, 'ctx', self.swap)  4.71 us
    ppermute x19, waiting for transfers between devices, go_mate(): return lax.ppermute(block, 'ctx', self.swap)  4.68 us
    pallas_call x1, Pallas kernels, attend(): pl.pallas_call(functools.partial(attention_kernel, count, heads, head_dim...  3.83 us
  transfers between devices with their start and end apart: 49, of which 23 were waited for; matrix products, arithmetic and copies ran while one was open for 12% of the time, Pallas kernels for 19%

profile of v1, /device:TPU:0, one launch (start us, length us, event | category | flops | bytes accessed | tf_op | source)
XLA Modules:
  0.0 189.9 jit_solution(5837087394491829558)
XLA Ops:
  1.0 3.6 %collective-permute-start.2 = (bf16[128,128]{1,0:T(8,128)(2,1)}, bf16[128,128]{1,0:T(8,128)(2,1)S(1)}, u32[]{:S(2)}, u32[]{:S(2)}) collective-permute-start(bf16[128,128]{1,0:T(8,128)(2,1)} %refs_0_.1), channel_id=1, source_target_pairs={{0,8},{1,9},{4,12},{5,13},{8,14},{9,15},{12,10},{13,11},{14,6},{15... | collective-permute-start | bytes 98312 | tf_op jit(solution)/shard_map/ppermute | solution.py:39
  4.6 2.2 %collective-permute-done.2.refs_3_ = bf16[128,128]{1,0:T(8,128)(2,1)S(1)} collective-permute-done((bf16[128,128]{1,0:T(8,128)(2,1)}, bf16[128,128]{1,0:T(8,128)(2,1)S(1)}, u32[]{:S(2)}, u32[]{:S(2)}) %collective-permute-start.2) | collective-permute-done | bytes 32800 | tf_op jit(solution)/shard_map/ppermute | solution.py:39
  6.8 4.3 %collective-permute-start.4 = (bf16[128,128]{1,0:T(8,128)(2,1)}, bf16[128,128]{1,0:T(8,128)(2,1)S(1)}, u32[]{:S(2)}, u32[]{:S(2)}) collective-permute-start(bf16[128,128]{1,0:T(8,128)(2,1)} %refs_0_.1), channel_id=1, source_target_pairs={{0,12},{1,13},{4,14},{5,15},{8,10},{9,11},{12,6},{13,7},{14,2},{15... | collective-permute-start | bytes 98312 | tf_op jit(solution)/shard_map/ppermute | solution.py:39
  11.1 2.0 %collective-permute-done.4.refs_5_ = bf16[128,128]{1,0:T(8,128)(2,1)S(1)} collective-permute-done((bf16[128,128]{1,0:T(8,128)(2,1)}, bf16[128,128]{1,0:T(8,128)(2,1)S(1)}, u32[]{:S(2)}, u32[]{:S(2)}) %collective-permute-start.4) | collective-permute-done | bytes 32800 | tf_op jit(solution)/shard_map/ppermute | solution.py:39
  13.0 5.8 %collective-permute-start.6 = (bf16[128,128]{1,0:T(8,128)(2,1)}, bf16[128,128]{1,0:T(8,128)(2,1)S(1)}, u32[]{:S(2)}, u32[]{:S(2)}) collective-permute-start(bf16[128,128]{1,0:T(8,128)(2,1)} %refs_0_.1), channel_id=1, source_target_pairs={{0,14},{1,15},{4,10},{5,11},{8,6},{9,7},{12,2},{13,3},{14,0},{15,1... | collective-permute-start | bytes 98312 | tf_op jit(solution)/shard_map/ppermute | solution.py:39
  18.9 2.1 %collective-permute-done.6.refs_7_ = bf16[128,128]{1,0:T(8,128)(2,1)S(1)} collective-permute-done((bf16[128,128]{1,0:T(8,128)(2,1)}, bf16[128,128]{1,0:T(8,128)(2,1)S(1)}, u32[]{:S(2)}, u32[]{:S(2)}) %collective-permute-start.6) | collective-permute-done | bytes 32800 | tf_op jit(solution)/shard_map/ppermute | solution.py:39
  23.4 2.1 %collective-permute-done.16.refs_18_ = bf16[128,128]{1,0:T(8,128)(2,1)S(1)} collective-permute-done((bf16[128,128]{1,0:T(8,128)(2,1)}, bf16[128,128]{1,0:T(8,128)(2,1)S(1)}, u32[]{:S(2)}, u32[]{:S(2)}) %collective-permute-start.16) | collective-permute-done | bytes 32800 | tf_op jit(solution)/shard_map/ppermute | solution.py:39
  26.3 3.0 %collective-permute-done.17.refs_19_ = bf16[128,128]{1,0:T(8,128)(2,1)S(1)} collective-permute-done((bf16[128,128]{1,0:T(8,128)(2,1)}, bf16[128,128]{1,0:T(8,128)(2,1)S(1)}, u32[]{:S(2)}, u32[]{:S(2)}) %collective-permute-start.17) | collective-permute-done | bytes 32800 | tf_op jit(solution)/shard_map/ppermute | solution.py:39
  30.9 2.6 %collective-permute-start.20 = (bf16[128,128]{1,0:T(8,128)(2,1)}, bf16[128,128]{1,0:T(8,128)(2,1)S(1)}, u32[]{:S(2)}, u32[]{:S(2)}) collective-permute-start(bf16[128,128]{1,0:T(8,128)(2,1)} %refs_16_.1), channel_id=1, source_target_pairs={{0,10},{1,11},{4,6},{5,7},{8,2},{9,3},{12,0},{13,1},{14,4},{15,5},... | collective-permute-start | bytes 98312 | tf_op jit(solution)/shard_map/ppermute | solution.py:39
  35.3 2.2 %collective-permute-start.21 = (bf16[128,128]{1,0:T(8,128)(2,1)}, bf16[128,128]{1,0:T(8,128)(2,1)S(1)}, u32[]{:S(2)}, u32[]{:S(2)}) collective-permute-start(bf16[128,128]{1,0:T(8,128)(2,1)} %refs_16_.1), channel_id=1, source_target_pairs={{0,14},{1,15},{4,10},{5,11},{8,6},{9,7},{12,2},{13,3},{14,0},{15,1... | collective-permute-start | bytes 98312 | tf_op jit(solution)/shard_map/ppermute | solution.py:39
  38.1 4.0 %collective-permute-done.21.refs_23_ = bf16[128,128]{1,0:T(8,128)(2,1)S(1)} collective-permute-done((bf16[128,128]{1,0:T(8,128)(2,1)}, bf16[128,128]{1,0:T(8,128)(2,1)S(1)}, u32[]{:S(2)}, u32[]{:S(2)}) %collective-permute-start.21) | collective-permute-done | bytes 32800 | tf_op jit(solution)/shard_map/ppermute | solution.py:39
  42.8 3.4 %collective-permute-done.1.refs_2_ = bf16[128,128]{1,0:T(8,128)(2,1)S(1)} collective-permute-done((bf16[128,128]{1,0:T(8,128)(2,1)}, bf16[128,128]{1,0:T(8,128)(2,1)S(1)}, u32[]{:S(2)}, u32[]{:S(2)}) %collective-permute-start.1) | collective-permute-done | bytes 32800 | tf_op jit(solution)/shard_map/ppermute | solution.py:39
  61.9 3.8 %attention.1 = (bf16[128,2048]{1,0:T(8,128)(2,1)S(1)}, bf16[128,2048]{1,0:T(8,128)(2,1)S(1)}) custom-call(s32[16]{0:T(128)S(1)} %dynamic-slice_bitcast_fusion.owner_ref, s32[16,4]{1,0:T(8,128)S(1)} %pad_add_fusion.edge_ref, bf16[128,1024]{1,0:T(8,128)(2,1)S(1)} %copy-done.16, bf16[128,2048]{1,0:T(8,128)(2,1)S(1)} %copy-done.3, f32[1,2048]{1,0:T(1,128)S(1)} %bitcast.9, ...), custom_call_target="tpu_custom_call" | custom-call | tf_op jit(solution)/shard_map/attention/pallas_call | solution.py:166
  68.5 12.0 %collective-permute-done.33.refs_0_ = bf16[128,2048]{1,0:T(8,128)(2,1)S(1)} collective-permute-done((bf16[128,2048]{1,0:T(8,128)(2,1)S(1)}, bf16[128,2048]{1,0:T(8,128)(2,1)S(1)}, u32[]{:S(2)}, u32[]{:S(2)}) %collective-permute-start.33) | collective-permute-done | bytes 524320 | tf_op jit(solution)/shard_map/ppermute | solution.py:39
  83.3 10.5 %collective-permute-done.34.refs_0_ = bf16[128,2048]{1,0:T(8,128)(2,1)S(1)} collective-permute-done((bf16[128,2048]{1,0:T(8,128)(2,1)S(1)}, bf16[128,2048]{1,0:T(8,128)(2,1)S(1)}, u32[]{:S(2)}, u32[]{:S(2)}) %collective-permute-start.34) | collective-permute-done | bytes 524320 | tf_op jit(solution)/shard_map/ppermute | solution.py:39
  97.4 9.2 %collective-permute-done.35.refs_0_ = bf16[128,2048]{1,0:T(8,128)(2,1)S(1)} collective-permute-done((bf16[128,2048]{1,0:T(8,128)(2,1)S(1)}, bf16[128,2048]{1,0:T(8,128)(2,1)S(1)}, u32[]{:S(2)}, u32[]{:S(2)}) %collective-permute-start.35) | collective-permute-done | bytes 524320 | tf_op jit(solution)/shard_map/ppermute | solution.py:39
  110.9 4.8 %copy.50.refs_1_.refs_2_ = bf16[2048,688]{1,0:T(8,128)(2,1)} copy(bf16[2048,688]{0,1:T(8,128)(2,1)} %param.20) | data formatting | bytes 5636096 | tf_op args[6]
  115.7 2.8 %copy.51.refs_2_.refs_3_ = bf16[2048,688]{1,0:T(8,128)(2,1)} copy(bf16[2048,688]{0,1:T(8,128)(2,1)S(1)} %copy-done.22) | data formatting | bytes 5636096 | tf_op args[7]
  118.5 4.6 %copy.52.refs_4_.refs_5_ = bf16[2048,688]{1,0:T(8,128)(2,1)} copy(bf16[2048,688]{0,1:T(8,128)(2,1)} %collective-permute-done.30) | data formatting | bytes 5636096 | tf_op jit(solution)/shard_map/ppermute | solution.py:42
  123.1 4.8 %copy.53.refs_5_.refs_6_ = bf16[2048,688]{1,0:T(8,128)(2,1)} copy(bf16[2048,688]{0,1:T(8,128)(2,1)} %collective-permute-done.31) | data formatting | bytes 5636096 | tf_op jit(solution)/shard_map/ppermute | solution.py:42
  128.0 7.3 %feed_forward.6 = (bf16[64,2048]{1,0:T(8,128)(2,1)S(1)}, bf16[64,2048]{1,0:T(8,128)(2,1)S(1)}) custom-call(bf16[64,2048]{1,0:T(8,128)(2,1)} %collective-permute-done.36.refs_0_, bf16[64,2048]{1,0:T(8,128)(2,1)} %collective-permute-done.40.refs_1_, bf16[2048,688]{1,0:T(8,128)(2,1)} %copy.50.refs_1_.refs_2_, bf16[2048,688]{1,0:T(8,128)(2,1)} %copy.51.refs_2_.refs_3_, ...), custom_call_target="tpu_custom_call" | custom-call | flops 2164260864 | bytes 16908288 | tf_op jit(solution)/shard_map/feed_forward/pallas_call | solution.py:236
  135.3 1.8 collective-permute-start.41
  137.1 8.9 %feed_forward.7 = (bf16[128,2048]{1,0:T(8,128)(2,1)S(1)}, bf16[128,2048]{1,0:T(8,128)(2,1)S(1)}) custom-call(bf16[128,2048]{1,0:T(8,128)(2,1)S(1)} %collective-permute-done.35.refs_0_, bf16[128,2048]{1,0:T(8,128)(2,1)S(1)} %copy-done.2, bf16[2048,688]{1,0:T(8,128)(2,1)} %copy.50.refs_1_.refs_2_, bf16[2048,688]{1,0:T(8,128)(2,1)} %copy.51.refs_2_.refs_3_, ...), custom_call_target="tpu_custom_call" | custom-call | flops 4328521728 | bytes 16908288 | tf_op jit(solution)/shard_map/feed_forward/pallas_call | solution.py:236
  146.5 1.8 collective-permute-start.42
  148.3 5.0 %collective-permute-done.45 = bf16[64,2048]{1,0:T(8,128)(2,1)S(1)} collective-permute-done((bf16[64,2048]{1,0:T(8,128)(2,1)S(1)}, bf16[64,2048]{1,0:T(8,128)(2,1)S(1)}, u32[]{:S(2)}, u32[]{:S(2)}) %collective-permute-start.45) | collective-permute-done | bytes 262176 | tf_op jit(solution)/shard_map/ppermute | solution.py:39
  153.9 8.9 %feed_forward.8 = (bf16[128,2048]{1,0:T(8,128)(2,1)S(1)}, bf16[128,2048]{1,0:T(8,128)(2,1)S(1)}) custom-call(bf16[128,2048]{1,0:T(8,128)(2,1)S(1)} %copy-done.11, bf16[128,2048]{1,0:T(8,128)(2,1)S(1)} %copy-done.13, bf16[2048,688]{1,0:T(8,128)(2,1)} %copy.50.refs_1_.refs_2_, bf16[2048,688]{1,0:T(8,128)(2,1)} %copy.51.refs_2_.refs_3_, ...), custom_call_target="tpu_custom_call" | custom-call | flops 4328521728 | bytes 16908288 | tf_op jit(solution)/shard_map/feed_forward/pallas_call | solution.py:236
  162.9 1.9 collective-permute-start.43
  165.4 8.9 %feed_forward.9 = (bf16[128,2048]{1,0:T(8,128)(2,1)S(1)}, bf16[128,2048]{1,0:T(8,128)(2,1)S(1)}) custom-call(bf16[128,2048]{1,0:T(8,128)(2,1)S(1)} %copy-done.7, bf16[128,2048]{1,0:T(8,128)(2,1)S(1)} %copy-done.9, bf16[2048,688]{1,0:T(8,128)(2,1)} %copy.50.refs_1_.refs_2_, bf16[2048,688]{1,0:T(8,128)(2,1)} %copy.51.refs_2_.refs_3_, ...), custom_call_target="tpu_custom_call" | custom-call | flops 4328521728 | bytes 16908288 | tf_op jit(solution)/shard_map/feed_forward/pallas_call | solution.py:236
  175.2 1.8 collective-permute-start.44
  179.0 6.2 %feed_forward.5 = bf16[128,2048]{1,0:T(8,128)(2,1)S(1)} custom-call(bf16[128,2048]{1,0:T(8,128)(2,1)S(1)} %copy-done.5, bf16[2048,688]{1,0:T(8,128)(2,1)} %copy.50.refs_1_.refs_2_, bf16[2048,688]{1,0:T(8,128)(2,1)} %copy.51.refs_2_.refs_3_, bf16[688,2048]{1,0:T(8,128)(2,1)S(1)} %copy-done, bf16[2048,688]{1,0:T(8,128)(2,1)} %copy.52.refs_4_.refs_5_, ...), custom_call_target="tpu_custom_call" | custom-call | flops 2164260864 | bytes 16908288 | tf_op jit(solution)/shard_map/feed_forward/pallas_call | solution.py:236
  185.2 2.2 %collective-permute-done.48 = bf16[128,2048]{1,0:T(8,128)(2,1)} collective-permute-done((bf16[128,2048]{1,0:T(8,128)(2,1)}, bf16[128,2048]{1,0:T(8,128)(2,1)}, u32[]{:S(2)}, u32[]{:S(2)}) %collective-permute-start.48) | collective-permute-done | bytes 524320 | tf_op jit(solution)/shard_map/ppermute | solution.py:39
  187.5 2.4 %add_convert_fusion = bf16[128,2048]{1,0:T(8,128)(2,1)} fusion(bf16[128,2048]{1,0:T(8,128)(2,1)S(1)} %copy-done.15, bf16[128,2048]{1,0:T(8,128)(2,1)} %collective-permute-done.48, bf16[128,2048]{1,0:T(8,128)(2,1)} %collective-permute-done.44, bf16[128,2048]{1,0:T(8,128)(2,1)S(1)} %feed_forward.5, f32[128]{0:T(128)S(1)} %compare_convert_fusion), kind=kLoop, calls=%fused_computation | loop fusion | flops 2883584 | bytes 2621952 | tf_op jit(solution)/shard_map/convert_element_type | solution.py:332
  (139 shorter events, 42.7 us)
Async XLA Ops:
  0.0 118.5 %collective-permute-start.30 = (bf16[2048,688]{0,1:T(8,128)(2,1)}, bf16[2048,688]{0,1:T(8,128)(2,1)}, u32[]{:S(2)}, u32[]{:S(2)}) collective-permute-start(bf16[2048,688]{0,1:T(8,128)(2,1)} %param.20), channel_id=1, source_target_pairs={{0,1},{1,0},{2,3},{3,2},{4,5},{5,4},{6,7},{7,6},{8,9},{9,8},{10,11... | collective-permute-start | bytes 8454152 | tf_op jit(solution)/shard_map/ppermute | solution.py:42
  0.5 122.7 %collective-permute-start.31 = (bf16[2048,688]{0,1:T(8,128)(2,1)}, bf16[2048,688]{0,1:T(8,128)(2,1)}, u32[]{:S(2)}, u32[]{:S(2)}) collective-permute-start(bf16[2048,688]{0,1:T(8,128)(2,1)} %param.21), channel_id=1, source_target_pairs={{0,1},{1,0},{2,3},{3,2},{4,5},{5,4},{6,7},{7,6},{8,9},{9,8},{10,11... | collective-permute-start | bytes 8454152 | tf_op jit(solution)/shard_map/ppermute | solution.py:42
  0.5 127.4 %collective-permute-start.32 = (bf16[688,2048]{1,0:T(8,128)(2,1)}, bf16[688,2048]{1,0:T(8,128)(2,1)}, u32[]{:S(2)}, u32[]{:S(2)}) collective-permute-start(bf16[688,2048]{1,0:T(8,128)(2,1)} %refs_4_.7), channel_id=1, source_target_pairs={{0,1},{1,0},{2,3},{3,2},{4,5},{5,4},{6,7},{7,6},{8,9},{9,8},{10,11... | collective-permute-start | bytes 8454152 | tf_op jit(solution)/shard_map/ppermute | solution.py:42
  1.0 5.8 %collective-permute-start.2 = (bf16[128,128]{1,0:T(8,128)(2,1)}, bf16[128,128]{1,0:T(8,128)(2,1)S(1)}, u32[]{:S(2)}, u32[]{:S(2)}) collective-permute-start(bf16[128,128]{1,0:T(8,128)(2,1)} %refs_0_.1), channel_id=1, source_target_pairs={{0,8},{1,9},{4,12},{5,13},{8,14},{9,15},{12,10},{13,11},{14,6},{15... | collective-permute-start | bytes 98312 | tf_op jit(solution)/shard_map/ppermute | solution.py:39
  4.6 6.5 %collective-permute-start.3 = (bf16[128,128]{1,0:T(8,128)(2,1)}, bf16[128,128]{1,0:T(8,128)(2,1)S(1)}, u32[]{:S(2)}, u32[]{:S(2)}) collective-permute-start(bf16[128,128]{1,0:T(8,128)(2,1)} %refs_0_.1), channel_id=1, source_target_pairs={{0,6},{1,7},{4,2},{5,3},{8,0},{9,1},{12,4},{13,5},{14,8},{15,9},{1... | collective-permute-start | bytes 98312 | tf_op jit(solution)/shard_map/ppermute | solution.py:39
  6.8 6.3 %collective-permute-start.4 = (bf16[128,128]{1,0:T(8,128)(2,1)}, bf16[128,128]{1,0:T(8,128)(2,1)S(1)}, u32[]{:S(2)}, u32[]{:S(2)}) collective-permute-start(bf16[128,128]{1,0:T(8,128)(2,1)} %refs_0_.1), channel_id=1, source_target_pairs={{0,12},{1,13},{4,14},{5,15},{8,10},{9,11},{12,6},{13,7},{14,2},{15... | collective-permute-start | bytes 98312 | tf_op jit(solution)/shard_map/ppermute | solution.py:39
  11.1 7.8 %collective-permute-start.5 = (bf16[128,128]{1,0:T(8,128)(2,1)}, bf16[128,128]{1,0:T(8,128)(2,1)S(1)}, u32[]{:S(2)}, u32[]{:S(2)}) collective-permute-start(bf16[128,128]{1,0:T(8,128)(2,1)} %refs_0_.1), channel_id=1, source_target_pairs={{0,10},{1,11},{4,6},{5,7},{8,2},{9,3},{12,0},{13,1},{14,4},{15,5},... | collective-permute-start | bytes 98312 | tf_op jit(solution)/shard_map/ppermute | solution.py:39
  13.0 8.0 %collective-permute-start.6 = (bf16[128,128]{1,0:T(8,128)(2,1)}, bf16[128,128]{1,0:T(8,128)(2,1)S(1)}, u32[]{:S(2)}, u32[]{:S(2)}) collective-permute-start(bf16[128,128]{1,0:T(8,128)(2,1)} %refs_0_.1), channel_id=1, source_target_pairs={{0,14},{1,15},{4,10},{5,11},{8,6},{9,7},{12,2},{13,3},{14,0},{15,1... | collective-permute-start | bytes 98312 | tf_op jit(solution)/shard_map/ppermute | solution.py:39
  18.9 4.5 %collective-permute-start.15 = (bf16[128,128]{1,0:T(8,128)(2,1)}, bf16[128,128]{1,0:T(8,128)(2,1)S(1)}, u32[]{:S(2)}, u32[]{:S(2)}) collective-permute-start(bf16[128,128]{1,0:T(8,128)(2,1)} %refs_16_.1), channel_id=1, source_target_pairs={{0,4},{1,5},{4,8},{5,9},{8,12},{9,13},{12,14},{13,15},{14,10},{15,... | collective-permute-start | bytes 98312 | tf_op jit(solution)/shard_map/ppermute | solution.py:39
  21.0 4.5 %collective-permute-start.16 = (bf16[128,128]{1,0:T(8,128)(2,1)}, bf16[128,128]{1,0:T(8,128)(2,1)S(1)}, u32[]{:S(2)}, u32[]{:S(2)}) collective-permute-start(bf16[128,128]{1,0:T(8,128)(2,1)} %refs_16_.1), channel_id=1, source_target_pairs={{0,2},{1,3},{4,0},{5,1},{8,4},{9,5},{12,8},{13,9},{14,12},{15,13},... | collective-permute-start | bytes 98312 | tf_op jit(solution)/shard_map/ppermute | solution.py:39
  23.4 5.9 %collective-permute-start.17 = (bf16[128,128]{1,0:T(8,128)(2,1)}, bf16[128,128]{1,0:T(8,128)(2,1)S(1)}, u32[]{:S(2)}, u32[]{:S(2)}) collective-permute-start(bf16[128,128]{1,0:T(8,128)(2,1)} %refs_16_.1), channel_id=1, source_target_pairs={{0,8},{1,9},{4,12},{5,13},{8,14},{9,15},{12,10},{13,11},{14,6},{15... | collective-permute-start | bytes 98312 | tf_op jit(solution)/shard_map/ppermute | solution.py:39
  25.5 5.4 %collective-permute-start.18 = (bf16[128,128]{1,0:T(8,128)(2,1)}, bf16[128,128]{1,0:T(8,128)(2,1)S(1)}, u32[]{:S(2)}, u32[]{:S(2)}) collective-permute-start(bf16[128,128]{1,0:T(8,128)(2,1)} %refs_16_.1), channel_id=1, source_target_pairs={{0,6},{1,7},{4,2},{5,3},{8,0},{9,1},{12,4},{13,5},{14,8},{15,9},{1... | collective-permute-start | bytes 98312 | tf_op jit(solution)/shard_map/ppermute | solution.py:39
  29.2 6.0 %collective-permute-start.19 = (bf16[128,128]{1,0:T(8,128)(2,1)}, bf16[128,128]{1,0:T(8,128)(2,1)S(1)}, u32[]{:S(2)}, u32[]{:S(2)}) collective-permute-start(bf16[128,128]{1,0:T(8,128)(2,1)} %refs_16_.1), channel_id=1, source_target_pairs={{0,12},{1,13},{4,14},{5,15},{8,10},{9,11},{12,6},{13,7},{14,2},{15... | collective-permute-start | bytes 98312 | tf_op jit(solution)/shard_map/ppermute | solution.py:39
  30.9 6.6 %collective-permute-start.20 = (bf16[128,128]{1,0:T(8,128)(2,1)}, bf16[128,128]{1,0:T(8,128)(2,1)S(1)}, u32[]{:S(2)}, u32[]{:S(2)}) collective-permute-start(bf16[128,128]{1,0:T(8,128)(2,1)} %refs_16_.1), channel_id=1, source_target_pairs={{0,10},{1,11},{4,6},{5,7},{8,2},{9,3},{12,0},{13,1},{14,4},{15,5},... | collective-permute-start | bytes 98312 | tf_op jit(solution)/shard_map/ppermute | solution.py:39
  35.3 6.8 %collective-permute-start.21 = (bf16[128,128]{1,0:T(8,128)(2,1)}, bf16[128,128]{1,0:T(8,128)(2,1)S(1)}, u32[]{:S(2)}, u32[]{:S(2)}) collective-permute-start(bf16[128,128]{1,0:T(8,128)(2,1)} %refs_16_.1), channel_id=1, source_target_pairs={{0,14},{1,15},{4,10},{5,11},{8,6},{9,7},{12,2},{13,3},{14,0},{15,1... | collective-permute-start | bytes 98312 | tf_op jit(solution)/shard_map/ppermute | solution.py:39
  37.5 5.3 %collective-permute-start = (bf16[128,128]{1,0:T(8,128)(2,1)}, bf16[128,128]{1,0:T(8,128)(2,1)S(1)}, u32[]{:S(2)}, u32[]{:S(2)}) collective-permute-start(bf16[128,128]{1,0:T(8,128)(2,1)} %refs_0_.1), channel_id=1, source_target_pairs={{0,4},{1,5},{4,8},{5,9},{8,12},{9,13},{12,14},{13,15},{14,10},{15,... | collective-permute-start | bytes 98312 | tf_op jit(solution)/shard_map/ppermute | solution.py:39
  66.5 14.0 %collective-permute-start.33 = (bf16[128,2048]{1,0:T(8,128)(2,1)S(1)}, bf16[128,2048]{1,0:T(8,128)(2,1)S(1)}, u32[]{:S(2)}, u32[]{:S(2)}) collective-permute-start(bf16[128,2048]{1,0:T(8,128)(2,1)S(1)} %get-tuple-element.16.refs_0_), channel_id=1, source_target_pairs={{0,4},{1,5},{4,8},{5,9},{8,12},{9,13},{12,14},{13,15},{14,10},{15,... | collective-permute-start | bytes 1572872 | tf_op jit(solution)/shard_map/ppermute | solution.py:39
  67.4 15.2 %collective-permute-start.37 = (bf16[128,2048]{1,0:T(8,128)(2,1)S(1)}, bf16[128,2048]{1,0:T(8,128)(2,1)S(1)}, u32[]{:S(2)}, u32[]{:S(2)}) collective-permute-start(bf16[128,2048]{1,0:T(8,128)(2,1)S(1)} %get-tuple-element.16.refs_0_), channel_id=1, source_target_pairs={{0,2},{1,3},{4,0},{5,1},{8,4},{9,5},{12,8},{13,9},{14,12},{15,13},... | collective-permute-start | bytes 1572872 | tf_op jit(solution)/shard_map/ppermute | solution.py:39
  80.5 13.3 %collective-permute-start.34 = (bf16[128,2048]{1,0:T(8,128)(2,1)S(1)}, bf16[128,2048]{1,0:T(8,128)(2,1)S(1)}, u32[]{:S(2)}, u32[]{:S(2)}) collective-permute-start(bf16[128,2048]{1,0:T(8,128)(2,1)S(1)} %collective-permute-done.33.refs_0_), channel_id=1, source_target_pairs={{0,4},{1,5},{4,8},{5,9},{8,12},{9,13},{12,14},{13,15},{14,10},{15,... | collective-permute-start | bytes 1572872 | tf_op jit(solution)/shard_map/ppermute | solution.py:39
  82.6 13.7 %collective-permute-start.38 = (bf16[128,2048]{1,0:T(8,128)(2,1)S(1)}, bf16[128,2048]{1,0:T(8,128)(2,1)S(1)}, u32[]{:S(2)}, u32[]{:S(2)}) collective-permute-start(bf16[128,2048]{1,0:T(8,128)(2,1)S(1)} %collective-permute-done.37.refs_1_), channel_id=1, source_target_pairs={{0,2},{1,3},{4,0},{5,1},{8,4},{9,5},{12,8},{13,9},{14,12},{15,13},... | collective-permute-start | bytes 1572872 | tf_op jit(solution)/shard_map/ppermute | solution.py:39
  93.8 12.9 %collective-permute-start.35 = (bf16[128,2048]{1,0:T(8,128)(2,1)S(1)}, bf16[128,2048]{1,0:T(8,128)(2,1)S(1)}, u32[]{:S(2)}, u32[]{:S(2)}) collective-permute-start(bf16[128,2048]{1,0:T(8,128)(2,1)S(1)} %collective-permute-done.34.refs_0_), channel_id=1, source_target_pairs={{0,4},{1,5},{4,8},{5,9},{8,12},{9,13},{12,14},{13,15},{14,10},{15,... | collective-permute-start | bytes 1572872 | tf_op jit(solution)/shard_map/ppermute | solution.py:39
  96.3 12.7 %collective-permute-start.39 = (bf16[128,2048]{1,0:T(8,128)(2,1)S(1)}, bf16[128,2048]{1,0:T(8,128)(2,1)S(1)}, u32[]{:S(2)}, u32[]{:S(2)}) collective-permute-start(bf16[128,2048]{1,0:T(8,128)(2,1)S(1)} %collective-permute-done.38.refs_1_), channel_id=1, source_target_pairs={{0,2},{1,3},{4,0},{5,1},{8,4},{9,5},{12,8},{13,9},{14,12},{15,13},... | collective-permute-start | bytes 1572872 | tf_op jit(solution)/shard_map/ppermute | solution.py:39
  107.4 20.6 %collective-permute-start.36 = (bf16[64,2048]{1,0:T(8,128)(2,1)}, bf16[64,2048]{1,0:T(8,128)(2,1)}, u32[]{:S(2)}, u32[]{:S(2)}) collective-permute-start(bf16[64,2048]{1,0:T(8,128)(2,1)} %slice.44), channel_id=1, source_target_pairs={{0,4},{1,5},{4,8},{5,9},{8,12},{9,13},{12,14},{13,15},{14,10},{15,... | collective-permute-start | bytes 786440 | tf_op jit(solution)/shard_map/ppermute | solution.py:39
  110.6 17.4 %collective-permute-start.40 = (bf16[64,2048]{1,0:T(8,128)(2,1)}, bf16[64,2048]{1,0:T(8,128)(2,1)}, u32[]{:S(2)}, u32[]{:S(2)}) collective-permute-start(bf16[64,2048]{1,0:T(8,128)(2,1)} %slice.45), channel_id=1, source_target_pairs={{0,2},{1,3},{4,0},{5,1},{8,4},{9,5},{12,8},{13,9},{14,12},{15,13},... | collective-permute-start | bytes 786440 | tf_op jit(solution)/shard_map/ppermute | solution.py:39
  135.3 11.1 %collective-permute-start.41 = (bf16[64,2048]{1,0:T(8,128)(2,1)S(1)}, bf16[64,2048]{1,0:T(8,128)(2,1)S(1)}, u32[]{:S(2)}, u32[]{:S(2)}) collective-permute-start(bf16[64,2048]{1,0:T(8,128)(2,1)S(1)} %get-tuple-element.17), channel_id=1, source_target_pairs={{0,2},{1,3},{4,0},{5,1},{8,4},{9,5},{12,8},{13,9},{14,12},{15,13},... | collective-permute-start | bytes 786440 | tf_op jit(solution)/shard_map/ppermute | solution.py:39
  146.0 7.3 %collective-permute-start.45 = (bf16[64,2048]{1,0:T(8,128)(2,1)S(1)}, bf16[64,2048]{1,0:T(8,128)(2,1)S(1)}, u32[]{:S(2)}, u32[]{:S(2)}) collective-permute-start(bf16[64,2048]{1,0:T(8,128)(2,1)S(1)} %get-tuple-element.22), channel_id=1, source_target_pairs={{0,4},{1,5},{4,8},{5,9},{8,12},{9,13},{12,14},{13,15},{14,10},{15,... | collective-permute-start | bytes 786440 | tf_op jit(solution)/shard_map/ppermute | solution.py:39
  146.5 16.3 %collective-permute-start.42 = (bf16[128,2048]{1,0:T(8,128)(2,1)S(1)}, bf16[128,2048]{1,0:T(8,128)(2,1)S(1)}, u32[]{:S(2)}, u32[]{:S(2)}) collective-permute-start(bf16[128,2048]{1,0:T(8,128)(2,1)S(1)} %pad_maximum_fusion), channel_id=1, source_target_pairs={{0,2},{1,3},{4,0},{5,1},{8,4},{9,5},{12,8},{13,9},{14,12},{15,13},... | collective-permute-start | bytes 1572872 | tf_op jit(solution)/shard_map/ppermute | solution.py:39
  153.4 11.6 %collective-permute-start.46 = (bf16[128,2048]{1,0:T(8,128)(2,1)S(1)}, bf16[128,2048]{1,0:T(8,128)(2,1)S(1)}, u32[]{:S(2)}, u32[]{:S(2)}) collective-permute-start(bf16[128,2048]{1,0:T(8,128)(2,1)S(1)} %pad_maximum_fusion.1), channel_id=1, source_target_pairs={{0,4},{1,5},{4,8},{5,9},{8,12},{9,13},{12,14},{13,15},{14,10},{15,... | collective-permute-start | bytes 1572872 | tf_op jit(solution)/shard_map/ppermute | solution.py:39
  162.9 11.4 %collective-permute-start.43 = (bf16[128,2048]{1,0:T(8,128)(2,1)S(1)}, bf16[128,2048]{1,0:T(8,128)(2,1)S(1)}, u32[]{:S(2)}, u32[]{:S(2)}) collective-permute-start(bf16[128,2048]{1,0:T(8,128)(2,1)S(1)} %add_convert_fusion.5), channel_id=1, source_target_pairs={{0,2},{1,3},{4,0},{5,1},{8,4},{9,5},{12,8},{13,9},{14,12},{15,13},... | collective-permute-start | bytes 1572872 | tf_op jit(solution)/shard_map/ppermute | solution.py:39
  165.1 11.9 %collective-permute-start.47 = (bf16[128,2048]{1,0:T(8,128)(2,1)S(1)}, bf16[128,2048]{1,0:T(8,128)(2,1)S(1)}, u32[]{:S(2)}, u32[]{:S(2)}) collective-permute-start(bf16[128,2048]{1,0:T(8,128)(2,1)S(1)} %add_convert_fusion.3), channel_id=1, source_target_pairs={{0,4},{1,5},{4,8},{5,9},{8,12},{9,13},{12,14},{13,15},{14,10},{15,... | collective-permute-start | bytes 1572872 | tf_op jit(solution)/shard_map/ppermute | solution.py:39
  175.2 10.0 %collective-permute-start.44 = (bf16[128,2048]{1,0:T(8,128)(2,1)}, bf16[128,2048]{1,0:T(8,128)(2,1)}, u32[]{:S(2)}, u32[]{:S(2)}) collective-permute-start(bf16[128,2048]{1,0:T(8,128)(2,1)} %add_convert_fusion.4), channel_id=1, source_target_pairs={{0,2},{1,3},{4,0},{5,1},{8,4},{9,5},{12,8},{13,9},{14,12},{15,13},... | collective-permute-start | bytes 1572872 | tf_op jit(solution)/shard_map/ppermute | solution.py:39
  178.0 9.5 %collective-permute-start.48 = (bf16[128,2048]{1,0:T(8,128)(2,1)}, bf16[128,2048]{1,0:T(8,128)(2,1)}, u32[]{:S(2)}, u32[]{:S(2)}) collective-permute-start(bf16[128,2048]{1,0:T(8,128)(2,1)} %add_convert_fusion.2), channel_id=1, source_target_pairs={{0,4},{1,5},{4,8},{5,9},{8,12},{9,13},{12,14},{13,15},{14,10},{15,... | collective-permute-start | bytes 1572872 | tf_op jit(solution)/shard_map/ppermute | solution.py:39
  (40 other events, 160.3 us)
